TPU v7x, 128 devices: a whole 4x4x4 slice. The times are simulated.
128 devices in a mesh: rows: 8 (over x, z_lo), cols: 16 (over z_hi, y, core).
Axes of the slice: x: 4, y: 4, z: 4 (z_hi: 2, z_lo: 2; z = z_hi * 2 + z_lo), core: 2. Of those that a mesh axis runs over, the one named last changes fastest.
Arguments:
- spectra: bfloat16 [4096, 4096], P(('rows', 'cols')), may hold values from -6 to 6
- band_weights: float32 [2048], replicated, may hold values from 0.3 to 3
- lag_weights: float32 [4], replicated, may hold values from 0.5 to 2
- selected_bins: int32 [8], replicated, may hold values from 0 to 31
Outputs:
- correlations: float32 [4, 4096, 4096], P(None, 'rows', 'cols')
- gradient: float32 [4096, 4096], P(('rows', 'cols'))
All inputs are finite; a program needn't handle non-finite values.
Results may differ from a plain program's by a relative error of at most 0.0045.
Values may be sent and summed in bfloat16 or wider, within the bound.
A program may use at most 128 MiB of HBM per device.

v0:
```python
import jax
import jax.numpy as jnp
from jax import lax
from jax.sharding import PartitionSpec as P

LAGS = 4
LAG_STEP = 8
BIN = 128


def spread(block, axis, owner):
    block = jnp.where(lax.axis_index(axis) == owner, block, jnp.zeros_like(block))
    return lax.psum(block, axis)


def per_device(spectra, band_weights, lag_weights, selected_bins):
    n_rows = lax.axis_size("rows")
    n_cols = lax.axis_size("cols")
    row_index = lax.axis_index("rows")
    col_index = lax.axis_index("cols")
    freqs = band_weights.shape[0]
    raw = spectra.astype(jnp.float32)
    mean_power = jnp.mean(raw * raw, axis=1, keepdims=True)
    bin_gains = jnp.concatenate([band_weights, band_weights])
    whitened = (raw * lax.rsqrt(mean_power + 1e-05) * bin_gains[None, :]).astype(jnp.bfloat16)
    row_tile = lax.all_gather(whitened, "cols", axis=0, tiled=True)
    row_len = row_tile.shape[0]
    fold_ratio = n_cols // n_rows
    col_len = row_len // fold_ratio
    slot_part = col_index % fold_ratio
    owner_row = col_index // fold_ratio
    own_piece = lax.dynamic_slice_in_dim(row_tile, slot_part * col_len, col_len, 0)
    col_tile = spread(own_piece, "rows", owner_row)
    row_chan = row_index * row_len + jnp.arange(row_len, dtype=jnp.int32)
    col_chan = col_index * col_len + jnp.arange(col_len, dtype=jnp.int32)
    distance = jnp.abs(row_chan[:, None] - col_chan[None, :]) // BIN
    selected = jnp.any(distance[:, :, None] == selected_bins[None, None, :], axis=2).astype(
        jnp.float32
    )
    norm_scale = 1.0 / jnp.sqrt(jnp.float32(2 * freqs))
    bin_index = jnp.arange(freqs, dtype=jnp.float32)
    real_part = row_tile[:, :freqs].astype(jnp.float32)
    imag_part = row_tile[:, freqs:].astype(jnp.float32)
    outputs = []
    row_grad = jnp.zeros((row_len, 2 * freqs), jnp.float32)
    col_grad = jnp.zeros((col_len, 2 * freqs), jnp.float32)
    for lag_index in range(LAGS):
        shift_lag = float((lag_index - LAGS // 2) * LAG_STEP)
        theta = jnp.pi * bin_index * shift_lag / freqs
        cosine = jnp.cos(theta)
        sine_part = jnp.sin(theta)
        rotated = jnp.concatenate(
            [
                real_part * cosine - imag_part * sine_part,
                imag_part * cosine + real_part * sine_part,
            ],
            axis=1,
        ).astype(jnp.bfloat16)
        correlation = (
            lax.dot_general(
                rotated, col_tile, (((1,), (1,)), ((), ())), preferred_element_type=jnp.float32
            )
            * norm_scale
        )
        outputs.append(correlation)
        adjoint = (lag_weights[lag_index] * selected * correlation).astype(jnp.bfloat16)
        back = jnp.dot(adjoint, col_tile, preferred_element_type=jnp.float32) * norm_scale
        back_real = back[:, :freqs]
        back_imag = back[:, freqs:]
        row_grad = row_grad + jnp.concatenate(
            [
                back_real * cosine + back_imag * sine_part,
                back_imag * cosine - back_real * sine_part,
            ],
            axis=1,
        )
        col_grad = (
            col_grad
            + lax.dot_general(
                adjoint, rotated, (((0,), (0,)), ((), ())), preferred_element_type=jnp.float32
            )
            * norm_scale
        )
    col_total = lax.psum(col_grad, "rows")
    is_owner = (owner_row == row_index).astype(jnp.float32)
    addition = lax.dynamic_update_slice_in_dim(
        jnp.zeros_like(row_grad), col_total * is_owner, slot_part * col_len, 0
    )
    gradient = lax.psum_scatter(row_grad + addition, "cols", scatter_dimension=0, tiled=True)
    return (jnp.stack(outputs), gradient)


def solution(mesh):
    placed = (P(("rows", "cols"), None), P(), P(), P())
    return jax.shard_map(
        per_device,
        mesh=mesh,
        in_specs=placed,
        out_specs=(P(None, "rows", "cols"), P(("rows", "cols"), None)),
        check_vma=False,
    )
```

profile of v0, /device:TPU:0, one launch (start us, length us, event | category | flops | bytes accessed | tf_op | source)
XLA Modules:
  0.0 497.7 jit_solution(1436570777540770167)
XLA Ops:
  7.2 0.0 copy-start.16
  7.2 0.0 all-gather.2.cloned.1.call-start
  7.2 1.1 fusion.28
  8.3 0.8 pad_maximum_fusion.21
  9.1 1.8 fusion.30
  10.9 0.0 all-gather.2.cloned.1.call-update
  10.9 0.0 all-reduce.3.cloned.1.call-start
  11.0 1.5 fusion.58
  12.5 0.1 fusion.40
  12.6 0.1 fusion.38
  12.6 0.1 fusion.36
  12.7 57.0 %all-gather.2.cloned.1.call-done = bf16[512,4096]{1,0:T(8,128)(2,1)} async-done(((bf16[32,4096]{1,0:T(8,128)(2,1)}), bf16[512,4096]{1,0:T(8,128)(2,1)}) %all-gather.2.cloned.1.call-update) | async-done | bytes 4194320 | tf_op jit(solution)/shard_map/all_gather | solution.py:26
  69.7 3.3 dynamic-slice_select_fusion
  73.0 0.0 all-reduce.3.cloned.1.call-update
  73.0 0.0 all-reduce.5.cloned.1.call-start
  73.1 0.1 fusion.34
  73.1 0.4 add_select_fusion
  73.6 0.0 copy-done.16
  73.6 1.7 compare_reduce_fusion
  75.3 0.0 copy-start.1
  75.3 6.1 %fusion.8 = (bf16[512,2048]{1,0:T(8,128)(2,1)}, bf16[512,2048]{1,0:T(8,128)(2,1)}) fusion(f32[2048]{0:T(1024)S(1)} %get-tuple-element.32, f32[2048]{0:T(1024)S(1)} %get-tuple-element.33, bf16[512,4096]{1,0:T(8,128)(2,1)} %all-gather.2.cloned.1.call-done), kind=kLoop, calls=%fused_computation.32 | loop fusion | flops 10485760 | bytes 8404992 | tf_op jit(solution)/shard_map/convert.4
  81.5 0.0 copy-done.1
  81.5 6.0 %fusion.4 = (bf16[512,2048]{1,0:T(8,128)(2,1)S(1)}, bf16[512,2048]{1,0:T(8,128)(2,1)}, bf16[512,2048]{1,0:T(8,128)(2,1)}, bf16[512,2048]{1,0:T(8,128)(2,1)}, bf1...) fusion(f32[2048]{0:T(1024)S(1)} %get-tuple-element.30, f32[2048]{0:T(1024)S(1)} %get-tuple-element.31, ...), kind=kLoop, calls=%fused_computation.28 | loop fusion | flops 27262976 | bytes 16826368 | tf_op jit(solution)/shard_map/convert.6
  87.5 89.1 %all-reduce.3.cloned.1.call-done = bf16[256,4096]{1,0:T(8,128)(2,1)} async-done(((bf16[256,4096]{1,0:T(8,128)(2,1)}), bf16[256,4096]{1,0:T(8,128)(2,1)}) %all-reduce.3.cloned.1.call-update) | async-done | bytes 2097168 | tf_op jit(solution)/shard_map/psum | solution.py:13
  176.5 3.7 fusion.24
  180.2 0.0 copy-done.11
  180.2 0.0 copy-start.13
  180.2 0.0 copy-done.12
  180.2 0.0 copy-start
  180.2 0.0 copy-start.6
  180.3 0.0 copy-start.7
  180.3 4.3 fusion.22
  184.6 0.0 copy-done.13
  184.6 0.0 copy-done
  184.6 1.3 fusion.25
  185.9 2.1 convolution_add_fusion.2
  188.0 0.1 copy-done.5
  188.1 1.3 fusion.26
  189.4 2.1 convolution_add_fusion.1
  191.6 0.1 copy-done.3
  191.7 1.3 fusion.27
  192.9 0.0 copy-start.8
  193.0 0.8 copy-done.8
  193.7 4.1 fusion.2
  197.9 0.0 all-reduce.5.cloned.1.call-update
  197.9 0.3 reduce-scatter.2.cloned.1.call-start
  198.2 0.0 copy-start.9
  198.2 5.2 %convolution_multiply_fusion.2 = f32[512,4096]{1,0:T(8,128)} fusion(bf16[256,4096]{1,0:T(8,128)(2,1)S(1)} %copy-done, f32[512,256]{1,0:T(8,128)S(1)} %fusion.25, pred[512,256]{1,0:T(8,128)(4,1)S(1)} %compare_reduce_fusion, f32[]{:T(128)} %bitcast.5), kind=kOutput, calls=%fused_computation.21 | convolution fusion | flops 1076232192 | bytes 11141124 | tf_op jit(solution)/shard_map/dot_general | solution.py:67
  203.4 0.0 copy-done.9
  203.4 5.2 %convolution_multiply_fusion = f32[512,4096]{1,0:T(8,128)} fusion(bf16[256,4096]{1,0:T(8,128)(2,1)S(1)} %copy-done, f32[512,256]{1,0:T(8,128)S(1)} %copy-done.9, pred[512,256]{1,0:T(8,128)(4,1)S(1)} %compare_reduce_fusion, f32[]{:T(128)} %bitcast.7), kind=kOutput, calls=%fused_computation.19 | convolution fusion | flops 1076232192 | bytes 11141124 | tf_op jit(solution)/shard_map/dot_general | solution.py:67
  208.6 2.0 convolution_multiply_fusion.1
  210.6 1.9 convolution_multiply_fusion.3
  212.5 8.8 %multiply_add_fusion.2 = (f32[512,2048]{1,0:T(8,128)}, f32[512,2048]{1,0:T(8,128)}) fusion(f32[512,4096]{1,0:T(8,128)} %convolution_multiply_fusion.2, f32[2048]{0:T(1024)S(1)} %get-tuple-element.32, f32[2048]{0:T(1024)S(1)} %get-tuple-element.33), kind=kLoop, calls=%fused_computation.53 | loop fusion | flops 6291456 | bytes 16793600 | tf_op jit(solution)/shard_map/add | solution.py:72
  221.2 8.8 %multiply_add_fusion = (f32[512,2048]{1,0:T(8,128)}, f32[512,2048]{1,0:T(8,128)}) fusion(f32[512,4096]{1,0:T(8,128)} %convolution_multiply_fusion, f32[2048]{0:T(1024)S(1)} %get-tuple-element.26, f32[2048]{0:T(1024)S(1)} %get-tuple-element.27), kind=kLoop, calls=%fused_computation.49 | loop fusion | flops 6291456 | bytes 16793600 | tf_op jit(solution)/shard_map/add | solution.py:72
  230.0 4.4 multiply_add_fusion.1
  234.4 4.5 multiply_add_fusion.3
  239.0 16.2 %fusion.1 = f32[512,4096]{1,0:T(8,128)} fusion(f32[512,2048]{1,0:T(8,128)} %get-tuple-element.9, f32[512,2048]{1,0:T(8,128)} %get-tuple-element.8, f32[512,2048]{1,0:T(8,128)} %get-tuple-element.7, f32[512,2048]{1,0:T(8,128)} %get-tuple-element.6, f32[512,2048]{1,0:T(8,128)} %get-tuple-element.5, f32[512,2048]{1,0:T(8,128)} %get-tuple-element.4, ...), kind=kLoop, calls=%fused_computation.18 | loop fusion | flops 14680064 | bytes 41943040 | tf_op jit(solution)/shard_map/add | solution.py:70
  255.2 124.5 %all-reduce.5.cloned.1.call-done = f32[256,4096]{1,0:T(8,128)} async-done(((f32[256,4096]{1,0:T(8,128)}), f32[256,4096]{1,0:T(8,128)}) %all-reduce.5.cloned.1.call-update) | async-done | bytes 4194320 | tf_op jit(solution)/shard_map/psum | solution.py:84
  379.7 6.2 %add_dynamic-update-slice_fusion = f32[512,4096]{1,0:T(8,128)} fusion(f32[512,4096]{1,0:T(8,128)} %fusion.1, s32[]{:T(128)S(6)} %select_n.35, f32[256,4096]{1,0:T(8,128)} %all-reduce.5.cloned.1.call-done, f32[]{:T(128)S(6)} %convert_element_type.40), kind=kLoop, calls=%fused_computation.47 | loop fusion | flops 2097152 | bytes 12582920 | tf_op jit(solution)/shard_map/add | solution.py:89
  385.9 0.0 reduce-scatter.2.cloned.1.call-update
  385.9 1.0 copy-done.10
  387.0 0.2 copy-done.15
  387.1 1.5 pad_maximum_fusion.12
  388.6 102.5 %reduce-scatter.2.cloned.1.call-done = f32[32,4096]{1,0:T(8,128)} async-done(((f32[512,4096]{1,0:T(8,128)}), f32[32,4096]{1,0:T(8,128)}) %reduce-scatter.2.cloned.1.call-update) | async-done | bytes 524304 | tf_op jit(solution)/shard_map/reduce_scatter | solution.py:89
  (17 shorter events, 0.0 us)
Async XLA Ops:
  7.2 66.4 %copy-start.16 = (s32[8]{0:T(128)S(1)}, s32[8]{0:T(128)}, u32[]{:S(2)}) copy-start(s32[8]{0:T(128)} %param.7) | copy-start | bytes 100
  7.2 62.5 %all-gather.2.cloned.1.call-start = ((), (), s32[]{:S(2)}) async-start(), calls=%async_computation.1 | async-start | bytes 4456448 | tf_op jit(solution)/shard_map/all_gather | solution.py:26
  10.9 165.6 %all-reduce.3.cloned.1.call-start = ((), (), s32[]{:S(2)}) async-start(), calls=%async_computation.2 | async-start | bytes 4194304 | tf_op jit(solution)/shard_map/psum | solution.py:13
  73.0 306.7 %all-reduce.5.cloned.1.call-start = ((), (), s32[]{:S(2)}) async-start(), calls=%async_computation.3 | async-start | bytes 8388608 | tf_op jit(solution)/shard_map/psum | solution.py:84
  75.3 6.1 %copy-start.1 = (bf16[512,4096]{1,0:T(8,128)(2,1)S(1)}, bf16[512,4096]{1,0:T(8,128)(2,1)}, u32[]{:S(2)}) copy-start(bf16[512,4096]{1,0:T(8,128)(2,1)} %all-gather.2.cloned.1.call-done) | copy-start | bytes 12582916
  87.5 92.7 %copy-start.11 = (bf16[512,2048]{1,0:T(8,128)(2,1)}, bf16[512,2048]{1,0:T(8,128)(2,1)S(1)}, u32[]{:S(2)}) copy-start(bf16[512,2048]{1,0:T(8,128)(2,1)S(1)} %get-tuple-element.10) | copy-start | bytes 6291460
  176.5 3.7 copy-start.12
  180.2 4.4 copy-start.13
  180.2 4.4 copy-start
  180.2 4.4 copy-start.6
  180.3 4.4 copy-start.7
  185.9 2.1 copy-start.4
  185.9 2.2 copy-start.5
  189.4 2.1 copy-start.2
  189.4 2.2 copy-start.3
  192.9 0.8 copy-start.8
  197.9 293.2 %reduce-scatter.2.cloned.1.call-start = ((), (), s32[]{:S(2)}) async-start(), calls=%async_computation.4 | async-start | bytes 8912896 | tf_op jit(solution)/shard_map/reduce_scatter | solution.py:89
  198.2 5.2 %copy-start.9 = (f32[512,256]{1,0:T(8,128)S(1)}, f32[512,256]{1,0:T(8,128)}, u32[]{:S(2)}) copy-start(f32[512,256]{1,0:T(8,128)} %copy-done.8) | copy-start | bytes 1572868
  208.6 2.0 copy-start.14
  385.9 1.0 copy-start.10
  385.9 1.2 copy-start.15
Sparse Core Ops, SparseCore 0:
  11.0 58.5 all-gather.1
  73.1 103.3 all-reduce.2
  198.0 181.6 all-reduce.4
  386.1 105.0 reduce-scatter.1
where the time goes:
time: 498 us
  waiting for transfers between devices  373 us (75%)
  other arithmetic  72 us (14%)
  matrix products  34.4 us (7%)
  between operations  14.1 us (3%)
    psum x1, waiting for transfers between devices, per_device(): col_total = lax.psum(col_grad, 'rows')  124 us
    reduce_scatter x1, waiting for transfers between devices, per_device(): lax.psum_scatter(row_grad + addition, 'cols', scatter_dimension=0, tiled=...  103 us
    psum x1, waiting for transfers between devices, spread(): return lax.psum(block, axis)  89.1 us
    all_gather x1, waiting for transfers between devices, per_device(): row_tile = lax.all_gather(whitened, 'cols', axis=0, tiled=True)  57 us
    add x4, other arithmetic, per_device(): back_real * cosine + back_imag * sine_part  26.5 us
    add x1, other arithmetic, per_device(): row_grad + jnp.concatenate([back_real * cosine + back_imag * sine_part, b...  16.2 us
    dot_general x4, matrix products, per_device(): jnp.dot(adjoint, col_tile, preferred_element_type=jnp.float32) * norm_scale  14.2 us
    dot_general x4, matrix products, per_device(): lax.dot_general(adjoint, rotated, (((0,), (0,)), ((), ())), preferred_ele...  12.6 us
  transfers between devices with their start and end apart: 4, of which 4 were waited for; matrix products, arithmetic and copies ran while one was open for 15% of the time, Pallas kernels for 0%

commit v1 on v0

--- a/solution.py
+++ b/solution.py
@@ -10,7 +10,7 @@
 
 def spread(block, axis, owner):
     block = jnp.where(lax.axis_index(axis) == owner, block, jnp.zeros_like(block))
-    return lax.psum(block, axis)
+    return jnp.sum(lax.all_gather(block, axis), axis=0)
 
 
 def per_device(spectra, band_weights, lag_weights, selected_bins):

time: 498 us -> 742 us (1.49)
  waiting for transfers between devices: 373 us -> 607 us
    all_gather x0 -> x1, waiting for transfers between devices: none -> 309 us  [spread(): return jnp.sum(lax.all_gather(block, axis), axis=0)]
    psum x1 -> x0, waiting for transfers between devices: 89.1 us -> none  [spread(): return lax.psum(block, axis)]
    psum x1, waiting for transfers between devices: 124 us -> 137 us  [per_device(): col_total = lax.psum(col_grad, 'rows')]
    reduce_sum x0 -> x1, other arithmetic: none -> 9.34 us  [spread(): return jnp.sum(lax.all_gather(block, axis), axis=0)]
    dot_general x4, matrix products: 14.2 us -> 22.2 us  [per_device(): jnp.dot(adjoint, col_tile, preferred_element_type=jnp.float32) * norm_scale]
  transfers between devices with their start and end apart: 4 -> 4, of which waited for: 4 -> 4; matrix products, arithmetic and copies ran while one was open for 15% -> 9% of each run, Pallas kernels for 0% -> 0%
where the time goes in v1:
time: 742 us
  waiting for transfers between devices  607 us (82%)
  other arithmetic  78.6 us (11%)
  matrix products  40 us (5%)
  between operations  14.1 us (2%)
    all_gather x1, waiting for transfers between devices, spread(): return jnp.sum(lax.all_gather(block, axis), axis=0)  309 us
    psum x1, waiting for transfers between devices, per_device(): col_total = lax.psum(col_grad, 'rows')  137 us
    reduce_scatter x1, waiting for transfers between devices, per_device(): lax.psum_scatter(row_grad + addition, 'cols', scatter_dimension=0, tiled=...  103 us
    all_gather x1, waiting for transfers between devices, per_device(): row_tile = lax.all_gather(whitened, 'cols', axis=0, tiled=True)  58.6 us
    add x4, other arithmetic, per_device(): back_real * cosine + back_imag * sine_part  23.3 us
    dot_general x4, matrix products, per_device(): jnp.dot(adjoint, col_tile, preferred_element_type=jnp.float32) * norm_scale  22.2 us
    add x1, other arithmetic, per_device(): row_grad + jnp.concatenate([back_real * cosine + back_imag * sine_part, b...  16.3 us
  transfers between devices with their start and end apart: 4, of which 4 were waited for; matrix products, arithmetic and copies ran while one was open for 9% of the time, Pallas kernels for 0%

profile of v1, /device:TPU:0, one launch (start us, length us, event | category | flops | bytes accessed | tf_op | source)
XLA Modules:
  0.0 741.9 jit_solution(11858983930458130918)
XLA Ops:
  7.2 0.0 copy-start.13
  7.2 0.0 copy-start.14
  7.2 0.0 all-gather.4.cloned.1.call-start
  7.2 1.1 fusion.28
  8.3 0.8 pad_maximum_fusion.21
  9.1 1.8 fusion.30
  10.9 0.0 all-gather.4.cloned.1.call-update
  10.9 0.0 all-gather.6.cloned.1.call-start
  11.0 58.6 %all-gather.4.cloned.1.call-done = bf16[512,4096]{1,0:T(8,128)(2,1)} async-done(((bf16[32,4096]{1,0:T(8,128)(2,1)}), bf16[512,4096]{1,0:T(8,128)(2,1)}) %all-gather.4.cloned.1.call-update) | async-done | bytes 4194320 | tf_op jit(solution)/shard_map/all_gather | solution.py:26
  69.7 3.3 dynamic-slice_select_fusion
  73.0 0.0 all-gather.6.cloned.1.call-update
  73.0 0.0 all-reduce.2.cloned.1.call-start
  73.1 0.0 copy-done.13
  73.1 0.7 fusion.58
  73.8 0.1 fusion.40
  73.8 0.1 fusion.38
  73.9 0.1 fusion.36
  73.9 0.1 fusion.34
  74.0 0.4 add_select_fusion
  74.4 0.0 copy-done.14
  74.4 1.7 compare_reduce_fusion
  76.2 0.0 copy-start
  76.2 6.1 fusion.8
  82.3 0.0 copy-done
  82.3 6.4 fusion.4
  88.7 308.8 %all-gather.6.cloned.1.call-done = bf16[2048,4096]{1,0:T(8,128)(2,1)} async-done(((bf16[256,4096]{1,0:T(8,128)(2,1)}), bf16[2048,4096]{1,0:T(8,128)(2,1)}) %all-gather.6.cloned.1.call-update) | async-done | bytes 16777232 | tf_op jit(solution)/shard_map/all_gather | solution.py:13
  397.5 9.3 %reduce_sum.22 = bf16[256,4096]{1,0:T(8,128)(2,1)S(1)} reduce(bf16[8,256,4096]{2,1,0:T(8,128)(2,1)} %bitcast.23, bf16[]{:T(256)} %constant.86.clone.1), dimensions={0}, to_apply=%region_1.2 | reduce | flops 7340032 | bytes 18874370 | tf_op jit(solution)/shard_map/reduce_sum | solution.py:13
  406.9 0.0 copy-start.9
  406.9 0.0 copy-start.10
  406.9 3.7 fusion.25
  410.6 1.3 fusion.24
  411.9 5.1 convolution_multiply_fusion.2
  417.0 2.1 fusion.22
  419.1 0.1 copy-done.6
  419.2 2.0 convolution_add_fusion.2
  421.3 0.2 copy-done.4
  421.4 1.3 fusion.26
  422.7 5.1 convolution_multiply_fusion.1
  427.8 2.0 convolution_add_fusion.1
  429.8 0.2 copy-done.2
  430.0 1.3 fusion.27
  431.3 0.0 copy-start.7
  431.3 5.4 convolution_multiply_fusion
  436.7 0.0 copy-done.7
  436.8 4.1 fusion.2
  440.8 0.0 all-reduce.2.cloned.1.call-update
  440.9 0.0 reduce-scatter.2.cloned.1.call-start
  440.9 0.0 slice-start.2
  440.9 6.6 convolution_multiply_fusion.3
  447.5 9.0 %multiply_add_fusion.2 = (f32[512,2048]{1,0:T(8,128)}, f32[512,2048]{1,0:T(8,128)}) fusion(f32[512,4096]{1,0:T(8,128)} %convolution_multiply_fusion.2, f32[2048]{0:T(1024)S(1)} %get-tuple-element.32, f32[2048]{0:T(1024)S(1)} %get-tuple-element.33), kind=kLoop, calls=%fused_computation.53 | loop fusion | flops 6291456 | bytes 16793600 | tf_op jit(solution)/shard_map/add | solution.py:72
  456.5 0.0 slice-done.3
  456.6 0.0 slice-start.4
  456.6 5.3 multiply_add_fusion
  461.9 4.5 multiply_add_fusion.1
  466.4 0.0 slice-done.4
  466.4 4.5 multiply_add_fusion.3
  470.8 16.3 %fusion.1 = f32[512,4096]{1,0:T(8,128)} fusion(f32[512,2048]{1,0:T(8,128)} %get-tuple-element.9, f32[512,2048]{1,0:T(8,128)} %get-tuple-element.8, f32[512,2048]{1,0:T(8,128)} %get-tuple-element.7, f32[512,2048]{1,0:T(8,128)} %get-tuple-element.6, f32[512,2048]{1,0:T(8,128)} %get-tuple-element.5, f32[512,2048]{1,0:T(8,128)} %get-tuple-element.4, ...), kind=kLoop, calls=%fused_computation.18 | loop fusion | flops 14680064 | bytes 41943040 | tf_op jit(solution)/shard_map/add | solution.py:70
  487.1 136.8 %all-reduce.2.cloned.1.call-done = f32[256,4096]{1,0:T(8,128)} async-done(((f32[256,4096]{1,0:T(8,128)}), f32[256,4096]{1,0:T(8,128)}) %all-reduce.2.cloned.1.call-update) | async-done | bytes 4194320 | tf_op jit(solution)/shard_map/psum | solution.py:84
  623.9 6.3 add_dynamic-update-slice_fusion
  630.2 0.0 reduce-scatter.2.cloned.1.call-update
  630.2 1.0 copy-done.8
  631.2 0.2 copy-done.12
  631.4 1.5 pad_maximum_fusion.12
  632.9 102.5 %reduce-scatter.2.cloned.1.call-done = f32[32,4096]{1,0:T(8,128)} async-done(((f32[512,4096]{1,0:T(8,128)}), f32[32,4096]{1,0:T(8,128)}) %reduce-scatter.2.cloned.1.call-update) | async-done | bytes 524304 | tf_op jit(solution)/shard_map/reduce_scatter | solution.py:89
  (29 shorter events, 0.1 us)
Async XLA Ops:
  7.2 65.9 %copy-start.13 = (f32[4]{0:T(128)S(1)}, f32[4]{0:T(128)}, u32[]{:S(2)}) copy-start(f32[4]{0:T(128)} %param.6) | copy-start | bytes 52
  7.2 67.3 %copy-start.14 = (s32[8]{0:T(128)S(1)}, s32[8]{0:T(128)}, u32[]{:S(2)}) copy-start(s32[8]{0:T(128)} %param.7) | copy-start | bytes 100
  7.2 62.5 %all-gather.4.cloned.1.call-start = ((), (), s32[]{:S(2)}) async-start(), calls=%async_computation.1 | async-start | bytes 4456448 | tf_op jit(solution)/shard_map/all_gather | solution.py:26
  10.9 386.6 %all-gather.6.cloned.1.call-start = ((), (), s32[]{:S(2)}) async-start(), calls=%async_computation.4 | async-start | bytes 18874368 | tf_op jit(solution)/shard_map/all_gather | solution.py:13
  73.0 550.9 %all-reduce.2.cloned.1.call-start = ((), (), s32[]{:S(2)}) async-start(), calls=%async_computation.2 | async-start | bytes 8388608 | tf_op jit(solution)/shard_map/psum | solution.py:84
  76.2 6.1 copy-start
  406.9 3.7 copy-start.9
  406.9 3.7 copy-start.10
  411.9 5.1 copy-start.11
  417.0 2.1 copy-start.5
  417.0 2.2 copy-start.6
  419.2 2.0 copy-start.3
  419.2 2.2 copy-start.4
  427.8 2.0 copy-start.1
  427.8 2.2 copy-start.2
  431.3 5.4 copy-start.7
  440.9 294.5 %reduce-scatter.2.cloned.1.call-start = ((), (), s32[]{:S(2)}) async-start(), calls=%async_computation.3 | async-start | bytes 8912896 | tf_op jit(solution)/shard_map/reduce_scatter | solution.py:89
  440.9 15.6 %slice-start.2 = ((s8[8388608]{0:T(1024)(128)(4,1)}), s8[4194304]{0:T(1024)(128)(4,1)S(1)}, s32[]{:S(2)}) async-start(s8[8388608]{0:T(1024)(128)(4,1)} %bitcast.19), calls=%async_computation.7 | async-start | bytes 8388608
  447.5 9.0 %slice-start.3 = ((s8[8388608]{0:T(1024)(128)(4,1)}), s8[4194304]{0:T(1024)(128)(4,1)S(1)}, s32[]{:S(2)}) async-start(s8[8388608]{0:T(1024)(128)(4,1)} %bitcast.19), calls=%async_computation.8 | async-start | bytes 8388608
  447.5 14.4 %slice-start = ((s8[8388608]{0:T(1024)(128)(4,1)}), s8[4194304]{0:T(1024)(128)(4,1)S(1)}, s32[]{:S(2)}) async-start(s8[8388608]{0:T(1024)(128)(4,1)} %bitcast.17), calls=%async_computation.5 | async-start | bytes 8388608
  456.5 5.3 slice-start.1
  456.6 9.8 %slice-start.4 = ((s8[8388608]{0:T(1024)(128)(4,1)}), s8[4194304]{0:T(1024)(128)(4,1)S(1)}, s32[]{:S(2)}) async-start(s8[8388608]{0:T(1024)(128)(4,1)} %bitcast.21), calls=%async_computation.9 | async-start | bytes 8388608
  461.9 4.5 slice-start.5
  630.2 1.0 copy-start.8
  630.2 1.2 copy-start.12
Sparse Core Ops, SparseCore 0:
  11.1 58.5 all-gather.3
  73.1 324.3 all-gather.5
  441.0 182.8 all-reduce.1
  630.3 105.0 reduce-scatter.1
